TPU v7x, 128 devices: a whole 4x4x4 slice. The times are simulated.
128 devices in a mesh: ctx: 16 (over z_hi, y, core), tp: 8 (over z_lo, x).
Axes of the slice: x: 4, y: 4, z: 4 (z_hi: 2, z_lo: 2; z = z_hi * 2 + z_lo), core: 2. Of those that a mesh axis runs over, the one named last changes fastest.
Arguments:
- queries: bfloat16 [1024, 8192], P('ctx', 'tp'), may hold values from -8 to 8
- cache_keys: bfloat16 [65536, 1024], P('ctx', 'tp'), may hold values from -8 to 8
- stored_values: bfloat16 [65536, 1024], P('ctx', 'tp'), may hold values from -6 to 6
- fresh_keys: bfloat16 [1024, 1024], P('ctx', 'tp'), may hold values from -12 to 12
- fresh_values: bfloat16 [1024, 1024], P('ctx', 'tp'), may hold values from -6 to 6
- positions: int32 [1024], P('ctx'), may hold values from 65536 to 66559, as said below
- lengths: int32 [16], P('ctx'), may hold values from 1024 to 4096, as said below
- out_weight: bfloat16 [8192, 8192], P('tp'), may hold values from -0.0625 to 0.0625
Outputs:
- attended_out: bfloat16 [1024, 8192], P('ctx', 'tp')
Inputs may be any that keep to these rules, and one draw needn't show every extreme that they name: A permutation of the positions that follow the cache: each of the values from min to max appears once. `lengths`: at least one shard is full in every draw.
All inputs are finite; a program needn't handle non-finite values.
Results may differ from a plain program's by a relative error of at most 0.015.
Values may be sent and summed in bfloat16 or wider, within the bound.
A program may use at most 128 MiB of HBM per device.

v0:
```python
import math

import jax
import jax.numpy as jnp
from jax import lax
from jax.sharding import PartitionSpec as P

QUERY_HEADS = 64
VALUE_HEADS_ALL = 8
HEAD_SIZE = 128


neg_large = -1e30


def attend_block(query_rows, key_rows, value_rows, valid_keys):
    kv_heads = query_rows.shape[1]
    head_dim = query_rows.shape[3]
    key_heads = key_rows.reshape(key_rows.shape[0], kv_heads, head_dim)
    value_heads = value_rows.reshape(value_rows.shape[0], kv_heads, head_dim)
    scores = jnp.einsum(
        "rkgd,ckd->rkgc", query_rows, key_heads, preferred_element_type=jnp.float32
    ) / math.sqrt(head_dim)
    key_mask = valid_keys[:, None, None, :]
    scores = jnp.where(key_mask, scores, neg_large)
    peak_now = jnp.max(scores, axis=3)
    weights = jnp.where(key_mask, jnp.exp(scores - peak_now[..., None]), 0.0)
    totals = jnp.sum(weights, axis=3)
    mixed_rows = jnp.einsum(
        "rkgc,ckd->rkgd",
        weights.astype(jnp.bfloat16),
        value_heads,
        preferred_element_type=jnp.float32,
    )
    return (mixed_rows / totals[..., None], peak_now + jnp.log(totals))


def merge_pair(out_first, log_first, out_second, log_second):
    upper_log = jnp.maximum(log_first, log_second)
    weight_first = jnp.exp(log_first - upper_log)
    weight_second = jnp.exp(log_second - upper_log)
    weight_total = weight_first + weight_second
    merged = (
        weight_first[..., None] * out_first + weight_second[..., None] * out_second
    ) / weight_total[..., None]
    return (merged, upper_log + jnp.log(weight_total))


def per_device(
    queries, cache_keys, stored_values, fresh_keys, fresh_values, positions, lengths, out_weight
):
    row_count = queries.shape[0]
    head_dim = HEAD_SIZE
    group_width = QUERY_HEADS // VALUE_HEADS_ALL
    kv_heads = cache_keys.shape[1] // head_dim
    cache_rows = cache_keys.shape[0]
    my_queries = queries.reshape(row_count, kv_heads, group_width, head_dim)
    all_positions, all_lengths = (
        lax.all_gather(positions, "ctx", axis=0, tiled=True),
        lax.all_gather(lengths, "ctx", axis=0, tiled=True),
    )
    all_turn_keys, all_turn_values = (
        lax.all_gather(fresh_keys, "ctx", axis=0, tiled=True),
        lax.all_gather(fresh_values, "ctx", axis=0, tiled=True),
    )
    turn_valid = all_positions[None, :] <= positions[:, None]
    turn_out, turn_log = attend_block(my_queries, all_turn_keys, all_turn_values, turn_valid)
    every_query = lax.all_gather(queries, "ctx", axis=0, tiled=True)
    total_rows = every_query.shape[0]
    block_rows = min(128, total_rows)
    grouped = every_query.reshape(
        total_rows // block_rows, block_rows, kv_heads, group_width, head_dim
    )
    local_valid = (jnp.arange(cache_rows, dtype=jnp.int32) < lengths[0])[None, :]

    def attend_local(query_block):
        return attend_block(query_block, cache_keys, stored_values, local_valid)

    block_out, block_log = lax.map(attend_local, grouped)
    head_count = kv_heads * group_width
    part_out = block_out.reshape(total_rows, head_count * head_dim)
    part_log = block_log.reshape(total_rows, head_count)
    back_out, back_log = (
        lax.all_to_all(part_out[None], "ctx", split_axis=1, concat_axis=0, tiled=True),
        lax.all_to_all(part_log[None], "ctx", split_axis=1, concat_axis=0, tiled=True),
    )
    source_count = back_log.shape[0]
    upper_log = jnp.max(back_log, axis=0)
    weights = jnp.exp(back_log - upper_log[None])
    weight_total = jnp.sum(weights, axis=0)
    weighted = jnp.sum(
        back_out.reshape(source_count, row_count, head_count, head_dim) * weights[..., None], axis=0
    )
    cache_out = (weighted / weight_total[..., None]).reshape(
        row_count, kv_heads, group_width, head_dim
    )
    cache_log = (upper_log + jnp.log(weight_total)).reshape(row_count, kv_heads, group_width)
    merged, unused_log = merge_pair(cache_out, cache_log, turn_out, turn_log)
    attended = merged.astype(jnp.bfloat16).reshape(row_count, kv_heads * group_width * head_dim)
    head_terms = jnp.dot(attended, out_weight, preferred_element_type=jnp.float32)
    return lax.psum_scatter(head_terms, "tp", scatter_dimension=1, tiled=True).astype(jnp.bfloat16)


def solution(mesh):
    placed = (
        P("ctx", "tp"),
        P("ctx", "tp"),
        P("ctx", "tp"),
        P("ctx", "tp"),
        P("ctx", "tp"),
        P("ctx"),
        P("ctx"),
        P("tp", None),
    )
    return jax.shard_map(
        per_device, mesh=mesh, in_specs=placed, out_specs=P("ctx", "tp"), check_vma=False
    )
```

profile of v0, /device:TPU:0, one launch (start us, length us, event | category | flops | bytes accessed | tf_op | source)
XLA Modules:
  0.0 372.4 jit_solution(2539123251253079379)
XLA Ops:
  6.5 0.7 all-gather.2.cloned.1.call-update
  7.3 53.5 %all-gather.2.cloned.1.call-done = bf16[1024,1024]{1,0:T(8,128)(2,1)} async-done(((bf16[64,1024]{1,0:T(8,128)(2,1)}), bf16[1024,1024]{1,0:T(8,128)(2,1)}) %all-gather.2.cloned.1.call-update) | async-done | bytes 2097168 | tf_op jit(solution)/shard_map/all_gather | solution.py:68
  60.8 2.2 copy.79
  63.0 104.6 %while.13 = (s32[]{:T(128)}, f32[8,128,1,8,128]{4,3,2,1,0:T(8,128)}, f32[8,128,1,8]{1,3,2,0:T(8,128)S(1)}, bf16[8,128,1,8,128]{4,3,1,0,2:T(8,128)(2,1)S(1)}, bf1...) while((s32[]{:T(128)}, f32[8,128,1,8,128]{4,3,2,1,0:T(8,128)}, ...), condition=%wide.region_3.4_spmd.clone, body=%wide.region_0.3_spmd.clone.sunk | while | flops 2202143744 | bytes 59032188 | solution.py:79
  63.0 0.7 iota_compare_fusion.2
  63.7 2.9 fusion.73
  66.6 4.9 %fusion.74 = f32[128,8]{0,1:T(8,128)S(1)} fusion(f32[128,8,4096]{2,0,1:T(8,128)S(1)} %get-tuple-element.172, f32[128,8]{0,1:T(8,128)S(1)} %get-tuple-element.173, pred[4096]{0:T(1024)(128)(4,1)S(1)} %iota_compare_fusion.2), kind=kLoop, calls=%fused_computation.5.clone.1 | loop fusion | flops 20970496 | bytes 16789504 | tf_op jit(solution)/shard_map/while/body/eval_jaxpr/reduce_sum | solution.py:28
  71.6 3.4 fusion.75
  75.0 1.1 copy_dynamic-update-slice_fusion.2
  76.1 0.7 iota_compare_fusion.2
  76.8 2.9 fusion.73
  79.7 4.9 %fusion.74 = f32[128,8]{0,1:T(8,128)S(1)} fusion(f32[128,8,4096]{2,0,1:T(8,128)S(1)} %get-tuple-element.172, f32[128,8]{0,1:T(8,128)S(1)} %get-tuple-element.173, pred[4096]{0:T(1024)(128)(4,1)S(1)} %iota_compare_fusion.2), kind=kLoop, calls=%fused_computation.5.clone.1 | loop fusion | flops 20970496 | bytes 16789504 | tf_op jit(solution)/shard_map/while/body/eval_jaxpr/reduce_sum | solution.py:28
  84.6 3.4 fusion.75
  88.0 1.1 copy_dynamic-update-slice_fusion.2
  89.2 0.7 iota_compare_fusion.2
  89.8 2.9 fusion.73
  92.8 4.9 %fusion.74 = f32[128,8]{0,1:T(8,128)S(1)} fusion(f32[128,8,4096]{2,0,1:T(8,128)S(1)} %get-tuple-element.172, f32[128,8]{0,1:T(8,128)S(1)} %get-tuple-element.173, pred[4096]{0:T(1024)(128)(4,1)S(1)} %iota_compare_fusion.2), kind=kLoop, calls=%fused_computation.5.clone.1 | loop fusion | flops 20970496 | bytes 16789504 | tf_op jit(solution)/shard_map/while/body/eval_jaxpr/reduce_sum | solution.py:28
  97.7 3.4 fusion.75
  101.1 1.1 copy_dynamic-update-slice_fusion.2
  102.3 0.7 iota_compare_fusion.2
  102.9 2.9 fusion.73
  105.9 4.9 %fusion.74 = f32[128,8]{0,1:T(8,128)S(1)} fusion(f32[128,8,4096]{2,0,1:T(8,128)S(1)} %get-tuple-element.172, f32[128,8]{0,1:T(8,128)S(1)} %get-tuple-element.173, pred[4096]{0:T(1024)(128)(4,1)S(1)} %iota_compare_fusion.2), kind=kLoop, calls=%fused_computation.5.clone.1 | loop fusion | flops 20970496 | bytes 16789504 | tf_op jit(solution)/shard_map/while/body/eval_jaxpr/reduce_sum | solution.py:28
  110.8 3.4 fusion.75
  114.2 1.1 copy_dynamic-update-slice_fusion.2
  115.3 0.7 iota_compare_fusion.2
  116.0 2.9 fusion.73
  118.9 4.9 %fusion.74 = f32[128,8]{0,1:T(8,128)S(1)} fusion(f32[128,8,4096]{2,0,1:T(8,128)S(1)} %get-tuple-element.172, f32[128,8]{0,1:T(8,128)S(1)} %get-tuple-element.173, pred[4096]{0:T(1024)(128)(4,1)S(1)} %iota_compare_fusion.2), kind=kLoop, calls=%fused_computation.5.clone.1 | loop fusion | flops 20970496 | bytes 16789504 | tf_op jit(solution)/shard_map/while/body/eval_jaxpr/reduce_sum | solution.py:28
  123.8 3.4 fusion.75
  127.3 1.1 copy_dynamic-update-slice_fusion.2
  128.4 0.7 iota_compare_fusion.2
  129.1 2.9 fusion.73
  132.0 4.9 %fusion.74 = f32[128,8]{0,1:T(8,128)S(1)} fusion(f32[128,8,4096]{2,0,1:T(8,128)S(1)} %get-tuple-element.172, f32[128,8]{0,1:T(8,128)S(1)} %get-tuple-element.173, pred[4096]{0:T(1024)(128)(4,1)S(1)} %iota_compare_fusion.2), kind=kLoop, calls=%fused_computation.5.clone.1 | loop fusion | flops 20970496 | bytes 16789504 | tf_op jit(solution)/shard_map/while/body/eval_jaxpr/reduce_sum | solution.py:28
  136.9 3.4 fusion.75
  140.3 1.1 copy_dynamic-update-slice_fusion.2
  141.5 0.7 iota_compare_fusion.2
  142.1 2.9 fusion.73
  145.1 4.9 %fusion.74 = f32[128,8]{0,1:T(8,128)S(1)} fusion(f32[128,8,4096]{2,0,1:T(8,128)S(1)} %get-tuple-element.172, f32[128,8]{0,1:T(8,128)S(1)} %get-tuple-element.173, pred[4096]{0:T(1024)(128)(4,1)S(1)} %iota_compare_fusion.2), kind=kLoop, calls=%fused_computation.5.clone.1 | loop fusion | flops 20970496 | bytes 16789504 | tf_op jit(solution)/shard_map/while/body/eval_jaxpr/reduce_sum | solution.py:28
  150.0 3.4 fusion.75
  153.4 1.1 copy_dynamic-update-slice_fusion.2
  154.5 0.7 iota_compare_fusion.2
  155.2 2.9 fusion.73
  158.1 4.9 %fusion.74 = f32[128,8]{0,1:T(8,128)S(1)} fusion(f32[128,8,4096]{2,0,1:T(8,128)S(1)} %get-tuple-element.172, f32[128,8]{0,1:T(8,128)S(1)} %get-tuple-element.173, pred[4096]{0:T(1024)(128)(4,1)S(1)} %iota_compare_fusion.2), kind=kLoop, calls=%fused_computation.5.clone.1 | loop fusion | flops 20970496 | bytes 16789504 | tf_op jit(solution)/shard_map/while/body/eval_jaxpr/reduce_sum | solution.py:28
  163.0 3.4 fusion.75
  166.5 1.1 copy_dynamic-update-slice_fusion.2
  167.6 0.3 copy.64
  167.9 0.5 broadcast.92
  168.4 1.9 reduce.5
  170.2 0.3 reshape.246
  170.5 11.2 %all_to_all.24 = f32[16,1,512]{2,1,0:T(1,128)S(1)} all-to-all(f32[16,1,512]{2,1,0:T(1,128)S(1)} %reshape.246), channel_id=1, replica_groups=mesh['ctx'=16,'tp'=8] {'ctx'}, dimensions={0} | all-to-all | bytes 65536 | tf_op jit(solution)/shard_map/all_to_all | solution.py:85
  181.8 4.7 %all-to-all-start.1 = ((f32[1,1024,1024]{2,0,1:T(1,128)}), f32[1,1024,1024]{2,0,1:T(1,128)}, u32[]{:S(2)}, u32[]{:S(2)}) async-start(f32[1,1024,1024]{2,0,1:T(1,128)} %bitcast.7), calls=%async_computation.1 | async-start | bytes 8388608 | tf_op jit(solution)/shard_map/all_to_all | solution.py:84
  186.5 0.6 dynamic-slice
  188.0 63.4 %all-reduce = s32[1024]{0:T(1024)S(1)} all-reduce(s32[1024]{0:T(1024)S(1)} %dynamic-update-slice), channel_id=1, replica_groups=mesh['ctx'=16,'tp'=8] {'ctx'}, use_global_device_ids=true, to_apply=%add | all-reduce | flops 1024 | bytes 8192
  251.4 22.3 %all_gather.14 = bf16[1024,128]{1,0:T(8,128)(2,1)S(1)} all-gather(bf16[64,128]{1,0:T(8,128)(2,1)S(1)} %copy-done.2), channel_id=1, replica_groups=mesh['ctx'=16,'tp'=8] {'ctx'}, dimensions={0}, use_global_device_ids=true | all-gather | bytes 278528 | tf_op jit(solution)/shard_map/all_gather | solution.py:63
  273.7 20.1 %all_gather.15 = bf16[1024,128]{1,0:T(8,128)(2,1)S(1)} all-gather(bf16[64,128]{1,0:T(8,128)(2,1)S(1)} %copy-done.3), channel_id=1, replica_groups=mesh['ctx'=16,'tp'=8] {'ctx'}, dimensions={0}, use_global_device_ids=true | all-gather | bytes 278528 | tf_op jit(solution)/shard_map/all_gather | solution.py:64
  294.0 0.6 fusion.30
  294.5 0.7 fusion.32
  295.2 0.6 reduce.6
  295.9 0.9 reshape.247
  297.1 2.6 mul.48
  299.7 10.0 %multiply_reduce_fusion = f32[64,1024]{1,0:T(8,128)S(1)} fusion(f32[1,16,64,1024]{3,0,2,1:T(1,128)} %bitcast.8, f32[1,16,64,1024]{3,0,2,1:T(1,128)} %bitcast.191), kind=kLoop, calls=%fused_computation.25 | loop fusion | flops 2031616 | bytes 8650752 | tf_op jit(solution)/shard_map/reduce_sum | solution.py:91
  309.7 0.7 fusion.38
  310.5 10.1 %fusion.50 = f32[64,8192]{1,0:T(8,128)} fusion(bf16[1024,8192]{1,0:T(8,128)(2,1)} %param.17, bf16[8,8,8,128]{3,2,1,0:T(8,128)(2,1)S(1)} %bitcast.198), kind=kOutput, calls=%fused_computation.50 | convolution fusion | flops 1073741824 | bytes 19005440 | tf_op jit(solution)/shard_map/dot_general | solution.py:100
  320.7 43.3 %reduce-scatter.2.cloned.1.call-done = f32[64,1024]{1,0:T(8,128)} async-done(((f32[64,8192]{1,0:T(8,128)}), f32[64,1024]{1,0:T(8,128)}) %reduce-scatter.2.cloned.1.call-update) | async-done | bytes 262160 | tf_op jit(solution)/shard_map/reduce_scatter | solution.py:101
  364.0 1.6 convert_element_type.14
  (60 shorter events, 1.2 us)
Async XLA Ops:
  6.5 56.5 %copy-start = (bf16[4096,128]{1,0:T(8,128)(2,1)S(1)}, bf16[4096,128]{1,0:T(8,128)(2,1)}, u32[]{:S(2)}) copy-start(bf16[4096,128]{1,0:T(8,128)(2,1)} %param.11) | copy-start | bytes 3145732
  6.5 54.2 %all-gather.2.cloned.1.call-start = ((), (), s32[]{:S(2)}) async-start(), calls=%async_computation.3 | async-start | bytes 2228224 | tf_op jit(solution)/shard_map/all_gather | solution.py:68
  66.6 4.9 %copy-start.5 = (bf16[4096,128]{1,0:T(8,128)(2,1)S(1)}, bf16[4096,128]{1,0:T(8,128)(2,1)}, u32[]{:S(2)}) copy-start(bf16[4096,128]{1,0:T(8,128)(2,1)} %get-tuple-element.195) | copy-start | bytes 3145732 | tf_op jit(solution)/shard_map/while
  79.7 4.9 %copy-start.5 = (bf16[4096,128]{1,0:T(8,128)(2,1)S(1)}, bf16[4096,128]{1,0:T(8,128)(2,1)}, u32[]{:S(2)}) copy-start(bf16[4096,128]{1,0:T(8,128)(2,1)} %get-tuple-element.195) | copy-start | bytes 3145732 | tf_op jit(solution)/shard_map/while
  92.8 4.9 %copy-start.5 = (bf16[4096,128]{1,0:T(8,128)(2,1)S(1)}, bf16[4096,128]{1,0:T(8,128)(2,1)}, u32[]{:S(2)}) copy-start(bf16[4096,128]{1,0:T(8,128)(2,1)} %get-tuple-element.195) | copy-start | bytes 3145732 | tf_op jit(solution)/shard_map/while
  105.8 4.9 %copy-start.5 = (bf16[4096,128]{1,0:T(8,128)(2,1)S(1)}, bf16[4096,128]{1,0:T(8,128)(2,1)}, u32[]{:S(2)}) copy-start(bf16[4096,128]{1,0:T(8,128)(2,1)} %get-tuple-element.195) | copy-start | bytes 3145732 | tf_op jit(solution)/shard_map/while
  118.9 4.9 %copy-start.5 = (bf16[4096,128]{1,0:T(8,128)(2,1)S(1)}, bf16[4096,128]{1,0:T(8,128)(2,1)}, u32[]{:S(2)}) copy-start(bf16[4096,128]{1,0:T(8,128)(2,1)} %get-tuple-element.195) | copy-start | bytes 3145732 | tf_op jit(solution)/shard_map/while
  132.0 4.9 %copy-start.5 = (bf16[4096,128]{1,0:T(8,128)(2,1)S(1)}, bf16[4096,128]{1,0:T(8,128)(2,1)}, u32[]{:S(2)}) copy-start(bf16[4096,128]{1,0:T(8,128)(2,1)} %get-tuple-element.195) | copy-start | bytes 3145732 | tf_op jit(solution)/shard_map/while
  145.1 4.9 %copy-start.5 = (bf16[4096,128]{1,0:T(8,128)(2,1)S(1)}, bf16[4096,128]{1,0:T(8,128)(2,1)}, u32[]{:S(2)}) copy-start(bf16[4096,128]{1,0:T(8,128)(2,1)} %get-tuple-element.195) | copy-start | bytes 3145732 | tf_op jit(solution)/shard_map/while
  158.1 4.9 %copy-start.5 = (bf16[4096,128]{1,0:T(8,128)(2,1)S(1)}, bf16[4096,128]{1,0:T(8,128)(2,1)}, u32[]{:S(2)}) copy-start(bf16[4096,128]{1,0:T(8,128)(2,1)} %get-tuple-element.195) | copy-start | bytes 3145732 | tf_op jit(solution)/shard_map/while
  181.8 4.8 %copy-start.6 = (u32[128]{0:T(128)S(1)}, u32[128]{0:T(128)}, u32[]{:S(2)}) copy-start(u32[128]{0:T(128)} %constant.36) | copy-start | bytes 1540
  181.8 6.0 %copy-start.4 = (s32[64]{0:T(128)S(1)}, s32[64]{0:T(128)}, u32[]{:S(2)}) copy-start(s32[64]{0:T(128)} %param.15) | copy-start | bytes 772
  181.8 69.6 %copy-start.2 = (bf16[64,128]{1,0:T(8,128)(2,1)S(1)}, bf16[64,128]{1,0:T(8,128)(2,1)}, u32[]{:S(2)}) copy-start(bf16[64,128]{1,0:T(8,128)(2,1)} %param.13) | copy-start | bytes 49156
  181.8 91.9 %copy-start.3 = (bf16[64,128]{1,0:T(8,128)(2,1)S(1)}, bf16[64,128]{1,0:T(8,128)(2,1)}, u32[]{:S(2)}) copy-start(bf16[64,128]{1,0:T(8,128)(2,1)} %param.14) | copy-start | bytes 49156
  181.8 112.2 %copy-start.1 = (bf16[64,1024]{1,0:T(8,128)(2,1)S(1)}, bf16[64,1024]{1,0:T(8,128)(2,1)}, u32[]{:S(2)}) copy-start(bf16[64,1024]{1,0:T(8,128)(2,1)} %param.10) | copy-start | bytes 393220
  181.8 115.3 %all-to-all-start.1 = ((f32[1,1024,1024]{2,0,1:T(1,128)}), f32[1,1024,1024]{2,0,1:T(1,128)}, u32[]{:S(2)}, u32[]{:S(2)}) async-start(f32[1,1024,1024]{2,0,1:T(1,128)} %bitcast.7), calls=%async_computation.1 | async-start | bytes 8388608 | tf_op jit(solution)/shard_map/all_to_all | solution.py:84
  186.5 177.5 %reduce-scatter.2.cloned.1.call-start = ((), (), s32[]{:S(2)}) async-start(), calls=%async_computation.4 | async-start | bytes 2359296 | tf_op jit(solution)/shard_map/reduce_scatter | solution.py:101
Sparse Core Ops, SparseCore 0:
  9.8 50.9 all-gather.1
  320.8 43.1 reduce-scatter.1
where the time goes:
time: 373 us; the launch traced here: 372 us
  blocking collectives  117 us (31%)
  waiting for transfers between devices  97.5 us (26%)
  matrix products  62.1 us (17%)
  other arithmetic  59.4 us (16%)
  local copies, waits for them, and re-layouts  17 us (5%)
  between operations  14.3 us (4%)
  starting transfers between devices  4.72 us (1%)
    unnamed x1, blocking collectives  63.4 us
    all_gather x1, waiting for transfers between devices, per_device(): every_query = lax.all_gather(queries, 'ctx', axis=0, tiled=True)  53.5 us
    reduce_scatter x1, waiting for transfers between devices, per_device(): lax.psum_scatter(head_terms, 'tp', scatter_dimension=1, tiled=True)  43.3 us
    reduce_sum x9, other arithmetic, attend_block(): totals = jnp.sum(weights, axis=3)  39.7 us
    dot_general x9, matrix products, attend_block(): jnp.einsum('rkgc,ckd->rkgd', weights.astype(jnp.bfloat16), value_heads, p...  28 us
    dot_general x9, matrix products, attend_block(): jnp.einsum('rkgd,ckd->rkgc', query_rows, key_heads, preferred_element_typ...  23.9 us
    all_gather x1, blocking collectives, per_device(): lax.all_gather(fresh_keys, 'ctx', axis=0, tiled=True)  22.3 us
    all_gather x1, blocking collectives, per_device(): lax.all_gather(fresh_values, 'ctx', axis=0, tiled=True)  20.1 us
  transfers between devices with their start and end apart: 3, of which 2 were waited for; matrix products, arithmetic and copies ran while one was open for 1% of the time, Pallas kernels for 0%

commit v1 on v0

v1 whole, which is shorter than its diff:
```python
import functools
import math

import jax
import jax.numpy as jnp
from jax import lax
from jax.experimental import pallas as pl
from jax.experimental.pallas import tpu as pltpu
from jax.sharding import PartitionSpec as P

HEAD = 128
GROUP = 8
FRESH = 128
BLOCKS = 4
LOW = -1e30
FAR = 1e9
ONES = 16
F32 = jnp.float32
BF16 = jnp.bfloat16
UNIT = math.log2(math.e) / math.sqrt(HEAD)
MESH = pl.DeviceIdType.MESH


def kernel(
    grid_ctx,
    grid_tp,
    q_ref,
    fk_ref,
    fv_ref,
    pos_ref,
    len_ref,
    k_hbm,
    v_hbm,
    w_hbm,
    out_ref,
    qbuf,
    meta,
    kbuf,
    vbuf,
    v_raw,
    wbuf,
    s_a,
    s_b,
    f_a,
    f_b,
    peak,
    m_now,
    acc,
    m_own,
    acc_own,
    part_out,
    part_log,
    got_out,
    got_log,
    attended,
    proj_out,
    proj_got,
    local_sem,
    q_send,
    q_recv,
    meta_send,
    meta_recv,
    kv_send,
    kv_recv,
    out_send,
    out_recv,
    log_send,
    log_recv,
    proj_send,
    proj_recv,
):
    nz, ny = grid_ctx
    tz, tx = grid_tp
    peers = nz * ny
    columns = tz * tx
    tokens = q_ref.shape[0]
    rows = tokens * GROUP
    slots = k_hbm.shape[0]
    block = slots // BLOCKS

    ctx = lax.axis_index("ctx")
    tp = lax.axis_index("tp")
    core = lax.rem(ctx, 2)
    chip = lax.div(ctx, 2)
    cz, cy = lax.div(chip, ny), lax.rem(chip, ny)
    pz, px = lax.div(tp, tx), lax.rem(tp, tx)
    partner = ctx + 1 - 2 * core

    def to_chip(k):
        z = lax.rem(cz + nz - lax.div(k, ny), nz)
        y = lax.rem(cy + ny - lax.rem(k, ny), ny)
        return (z * ny + y) * 2 + core

    def from_chip(k):
        z = lax.rem(cz + lax.div(k, ny), nz)
        y = lax.rem(cy + lax.rem(k, ny), ny)
        return (z * ny + y) * 2 + core

    def to_column(k):
        z = lax.rem(pz + lax.div(k, tx), tz)
        x = lax.rem(px + lax.rem(k, tx), tx)
        return z * tx + x

    def remote(src, dst, send, recv, where):
        return pltpu.make_async_remote_copy(
            src_ref=src, dst_ref=dst, send_sem=send, recv_sem=recv, device_id=where, device_id_type=MESH
        )

    def q_copy(k):
        return remote(qbuf.at[0], qbuf.at[k], q_send.at[k], q_recv.at[k], {"ctx": to_chip(k)})

    def meta_copy(k):
        return remote(meta.at[0], meta.at[k], meta_send.at[k], meta_recv.at[k], {"ctx": to_chip(k)})

    def meta_partner():
        return remote(meta.at[0], meta.at[peers], meta_send.at[peers], meta_recv.at[peers], {"ctx": partner})

    def k_partner():
        return remote(kbuf.at[0], kbuf.at[1], kv_send.at[0], kv_recv.at[0], {"ctx": partner})

    def v_partner():
        return remote(vbuf.at[0], vbuf.at[1], kv_send.at[1], kv_recv.at[1], {"ctx": partner})

    def out_copy(k):
        return remote(part_out.at[k], got_out.at[k], out_send.at[k], out_recv.at[k], {"ctx": from_chip(k)})

    def log_copy(k):
        return remote(part_log.at[k], got_log.at[k], log_send.at[k], log_recv.at[k], {"ctx": from_chip(k)})

    def proj_copy(k):
        return remote(proj_out.at[k], proj_got.at[k], proj_send.at[k], proj_recv.at[k], {"tp": to_column(k)})

    k_load = pltpu.make_async_copy(k_hbm, kbuf.at[0, pl.ds(0, slots)], local_sem.at[0])
    v_load = pltpu.make_async_copy(v_hbm, v_raw, local_sem.at[1])
    w_load = pltpu.make_async_copy(w_hbm, wbuf, local_sem.at[2])
    k_load.start()
    v_load.start()

    barrier = pltpu.get_barrier_semaphore()
    for k in range(1, peers):
        pl.semaphore_signal(barrier, inc=1, device_id={"ctx": to_chip(k)}, device_id_type=MESH)
    pl.semaphore_signal(barrier, inc=1, device_id={"ctx": partner}, device_id_type=MESH)
    for k in range(1, columns):
        pl.semaphore_signal(barrier, inc=1, device_id={"tp": to_column(k)}, device_id_type=MESH)

    stacked = jnp.concatenate([q_ref[:, h * HEAD : (h + 1) * HEAD].astype(F32) for h in range(GROUP)], axis=0)
    qbuf[0] = stacked.T.astype(BF16)
    meta[0] = jnp.broadcast_to(jnp.concatenate([pos_ref[...].astype(F32)] * GROUP, axis=1), (8, rows))
    spare = jnp.zeros((FRESH - tokens, HEAD), F32)
    kbuf[0, pl.ds(slots, FRESH), :] = jnp.concatenate([fk_ref[...].astype(F32), spare], axis=0).astype(BF16)
    vbuf[0, pl.ds(0, HEAD), pl.ds(slots, FRESH)] = (
        jnp.concatenate([fv_ref[...].astype(F32), spare], axis=0).T.astype(BF16)
    )
    vbuf[0, pl.ds(HEAD, ONES), pl.ds(slots, FRESH)] = jnp.ones((ONES, FRESH), BF16)

    pl.semaphore_wait(barrier, peers - 1 + 1 + columns - 1)
    first_sends = min(4, peers)
    for k in range(1, first_sends):
        q_copy(k).start()
    for k in range(1, peers):
        meta_copy(k).start()
    meta_partner().start()

    filled = len_ref[0]
    k_load.wait()
    lead = kbuf[0, pl.ds(0, 16), :].astype(F32)[0:1]
    tidy = block // 2

    @pl.loop(0, slots // tidy)
    def _(c):
        at = pl.ds(pl.multiple_of(c * tidy, tidy), tidy)
        valid = lax.broadcasted_iota(jnp.int32, (tidy, HEAD), 0) + c * tidy < filled
        kbuf[0, at, :] = jnp.where(valid, kbuf[0, at, :].astype(F32), lead).astype(BF16)

    k_partner().start()
    v_load.wait()

    @pl.loop(0, slots // tidy)
    def _(c):
        at = pl.ds(pl.multiple_of(c * tidy, tidy), tidy)
        valid = lax.broadcasted_iota(jnp.int32, (HEAD, tidy), 1) + c * tidy < filled
        vbuf[0, pl.ds(0, HEAD), at] = jnp.where(valid, v_raw[at, :].astype(F32).T, 0.0).astype(BF16)
        vbuf[0, pl.ds(HEAD, ONES), at] = jnp.where(valid[:ONES], 1.0, 0.0).astype(BF16)

    v_partner().start()
    w_load.start()

    def fresh_scores(tile, shard, fresh):
        row = lax.broadcasted_iota(jnp.int32, (FRESH, FRESH), 0)
        lane = lax.broadcasted_iota(jnp.int32, (FRESH, FRESH), 1)
        spots = jnp.where(row == lane, meta[shard * peers, 0:1, pl.ds(0, FRESH)], 0.0)
        spot = jnp.where(row[:, :1] < tokens, jnp.sum(spots, axis=1, keepdims=True), FAR)
        s = jnp.dot(kbuf[shard, pl.ds(slots, FRESH), :], qbuf[tile], preferred_element_type=F32)
        s = jnp.where(spot <= meta[tile, 0:1, :], s, LOW)
        fresh[...] = s
        return s

    wide = min(256, block)

    def top_of(s):
        return jnp.max(s.reshape(s.shape[0] // 8, 8, rows), axis=0)

    def phase(now, then, tile, shard_now, shard_then):
        if now is not None:
            s_now, f_now = now
            m_old = m_now[0:1, :]
            m_new = jnp.maximum(m_old, jnp.max(peak[...], axis=0, keepdims=True))
            fade = jnp.exp2((m_old - m_new) * UNIT)
            m_now[...] = jnp.broadcast_to(m_new, (8, rows))
            mk = m_new * UNIT
            p = jnp.exp2(f_now[...] * UNIT - mk).astype(BF16)
            add = jnp.dot(vbuf[shard_now, :, pl.ds(slots, FRESH)], p, preferred_element_type=F32)
            acc[...] = acc[...] * fade + add
        if then is not None:
            s_then, f_then = then
            top = top_of(fresh_scores(tile, shard_then, f_then))
        for b in range(BLOCKS):
            weights = []
            for c in range(block // wide):
                start = b * block + c * wide
                if then is not None:
                    s = jnp.dot(kbuf[shard_then, pl.ds(start, wide), :], qbuf[tile], preferred_element_type=F32)
                    s_then[pl.ds(start, wide), :] = s
                    top = jnp.maximum(top, top_of(s))
                if now is not None:
                    weights.append(jnp.exp2(s_now[pl.ds(start, wide), :] * UNIT - mk).astype(BF16))
            if now is not None:
                acc[...] += jnp.dot(
                    vbuf[shard_now, :, pl.ds(b * block, block)],
                    jnp.concatenate(weights, axis=0),
                    preferred_element_type=F32,
                )
        if then is not None:
            peak[...] = top

    def clear():
        acc[...] = jnp.zeros_like(acc)
        m_now[...] = jnp.full_like(m_now, LOW)

    def finish(k):
        total = acc[pl.ds(HEAD, 8), :]
        part_out[k] = (acc[pl.ds(0, HEAD), :] / total[0:1]).astype(BF16)
        part_log[k] = m_now[...] * UNIT + jnp.log(total) * math.log2(math.e)

    a, b = (s_a, f_a), (s_b, f_b)
    clear()
    phase(None, a, 0, None, 0)

    @pl.loop(0, peers)
    def _(t):
        shard = lax.rem(t, 2)
        tile = lax.rem(t + 1, peers)

        @pl.when(t + first_sends < peers)
        def _():
            q_copy(t + first_sends).start()

        @pl.when(t + 1 < peers)
        def _():
            q_copy(t + 1).wait_recv()
            meta_copy(t + 1).wait_recv()

        phase(a, b, tile, shard, shard)

        @pl.when(t == 0)
        def _():
            acc_own[...] = acc[...]
            m_own[...] = m_now[...]
            meta_partner().wait_recv()
            k_partner().wait_recv()

        @pl.when(t > 0)
        def _():
            finish(t)
            out_copy(t).start()
            log_copy(t).start()

        @pl.when(t + 1 < peers)
        def _():
            clear()
            phase(b, a, tile, shard, 1 - shard)

        @pl.when(t == 0)
        def _():
            v_partner().wait_recv()

        @pl.when(t + 1 == peers)
        def _():
            acc[...] = acc_own[...]
            m_now[...] = m_own[...]
            phase(b, None, None, shard, None)
            finish(0)

    for k in range(1, peers):
        out_copy(k).wait_recv()
        log_copy(k).wait_recv()
    logs = [part_log[0]] + [got_log[k] for k in range(1, peers)]
    top = functools.reduce(jnp.maximum, logs)
    shares = [jnp.exp2(log - top) for log in logs]
    whole = functools.reduce(jnp.add, shares)
    shares = [share / whole for share in shares]
    mixed = shares[0][0:1] * part_out[0].astype(F32)
    for k in range(1, peers):
        mixed += shares[k][0:1] * got_out[k].astype(F32)
    mixed = mixed.T.astype(BF16)
    for h in range(GROUP):
        attended[:, pl.ds(h * HEAD, HEAD)] = mixed[h * tokens : (h + 1) * tokens]

    w_load.wait()
    span = wbuf.shape[1] // columns

    def project(k):
        at = pl.ds(pl.multiple_of(to_column(k) * span, span), span)
        return jnp.dot(attended[...], wbuf[:, at], preferred_element_type=F32)

    @pl.loop(0, columns - 1)
    def _(s):
        k = columns - 1 - s
        proj_out[k] = project(k).astype(BF16)
        proj_copy(k).start()

    result = project(0)
    for k in range(columns - 1, 0, -1):
        proj_copy(k).wait_recv()
        result += proj_got[k].astype(F32)
    out_ref[...] = result.astype(BF16)

    for k in range(1, peers):
        q_copy(k).wait_send()
        meta_copy(k).wait_send()
        out_copy(k).wait_send()
        log_copy(k).wait_send()
    meta_partner().wait_send()
    k_partner().wait_send()
    v_partner().wait_send()
    for k in range(1, columns):
        proj_copy(k).wait_send()


def grid_of(count):
    return (2, count // 2) if count > 2 else (1, count)


def per_device(queries, cache_keys, stored_values, fresh_keys, fresh_values, positions, lengths, out_weight, sizes):
    ctx_size, tp_size = sizes
    grid_ctx, grid_tp = grid_of(ctx_size // 2), grid_of(tp_size)
    peers = ctx_size // 2
    tokens, width = queries.shape
    rows = tokens * GROUP
    slots = cache_keys.shape[0]
    span = out_weight.shape[1] // tp_size
    vmem = pl.BlockSpec(memory_space=pltpu.VMEM)
    anywhere = pl.BlockSpec(memory_space=pl.ANY)
    dma = pltpu.SemaphoreType.DMA
    return pl.pallas_call(
        functools.partial(kernel, grid_ctx, grid_tp),
        out_shape=jax.ShapeDtypeStruct((tokens, span), BF16),
        in_specs=[vmem, vmem, vmem, vmem, pl.BlockSpec(memory_space=pltpu.SMEM), anywhere, anywhere, anywhere],
        out_specs=vmem,
        scratch_shapes=[
            pltpu.VMEM((peers, HEAD, rows), BF16),
            pltpu.VMEM((peers + 1, 8, rows), F32),
            pltpu.VMEM((2, slots + FRESH, HEAD), BF16),
            pltpu.VMEM((2, HEAD + ONES, slots + FRESH), BF16),
            pltpu.VMEM((slots, HEAD), BF16),
            pltpu.VMEM(out_weight.shape, BF16),
            pltpu.VMEM((slots, rows), F32),
            pltpu.VMEM((slots, rows), F32),
            pltpu.VMEM((FRESH, rows), F32),
            pltpu.VMEM((FRESH, rows), F32),
            pltpu.VMEM((8, rows), F32),
            pltpu.VMEM((8, rows), F32),
            pltpu.VMEM((HEAD + ONES, rows), F32),
            pltpu.VMEM((8, rows), F32),
            pltpu.VMEM((HEAD + ONES, rows), F32),
            pltpu.VMEM((peers, HEAD, rows), BF16),
            pltpu.VMEM((peers, 8, rows), F32),
            pltpu.VMEM((peers, HEAD, rows), BF16),
            pltpu.VMEM((peers, 8, rows), F32),
            pltpu.VMEM((tokens, width), BF16),
            pltpu.VMEM((tp_size, tokens, span), BF16),
            pltpu.VMEM((tp_size, tokens, span), BF16),
            dma((3,)),
            dma((peers,)),
            dma((peers,)),
            dma((peers + 1,)),
            dma((peers + 1,)),
            dma((2,)),
            dma((2,)),
            dma((peers,)),
            dma((peers,)),
            dma((peers,)),
            dma((peers,)),
            dma((tp_size,)),
            dma((tp_size,)),
        ],
        compiler_params=pltpu.CompilerParams(
            collective_id=0, has_side_effects=True, vmem_limit_bytes=60 * 1024 * 1024
        ),
        cost_estimate=pl.CostEstimate(
            flops=4 * peers * rows * 2 * (slots + FRESH) * HEAD + 2 * tokens * width * out_weight.shape[1],
            bytes_accessed=2 * (out_weight.size + 2 * cache_keys.size),
            transcendentals=peers * rows * 2 * (slots + FRESH),
        ),
    )(
        queries,
        fresh_keys,
        fresh_values,
        positions.reshape(1, tokens),
        lengths,
        cache_keys,
        stored_values,
        out_weight,
    )


def solution(mesh):
    placed = (
        P("ctx", "tp"),
        P("ctx", "tp"),
        P("ctx", "tp"),
        P("ctx", "tp"),
        P("ctx", "tp"),
        P("ctx"),
        P("ctx"),
        P("tp", None),
    )
    sizes = (mesh.shape["ctx"], mesh.shape["tp"])
    return jax.shard_map(
        functools.partial(per_device, sizes=sizes),
        mesh=mesh,
        in_specs=placed,
        out_specs=P("ctx", "tp"),
        check_vma=False,
    )
```

time: 373 us -> 74.2 us (0.20)
  blocking collectives: 117 us -> 0 us
  waiting for transfers between devices: 97.5 us -> 0 us
  Pallas kernels: 0 us -> 70.7 us
  matrix products: 62.1 us -> 0 us
  other arithmetic: 59.4 us -> 0 us
  local copies, waits for them, and re-layouts: 17 us -> 1.57 us
  between operations: 14.3 us -> 0.66 us
  starting transfers between devices: 4.72 us -> 0 us
    pallas_call x0 -> x1, Pallas kernels: none -> 70.7 us  [per_device(): pl.pallas_call(functools.partial(kernel, grid_ctx, grid_tp), out_shape=ja...]
    unnamed x1 -> x0, blocking collectives: 63.4 us -> none
    dot_general x19 -> x0, matrix products: 62.1 us -> none  [the longest x9 28 us: attend_block(): jnp.einsum('rkgc,ckd->rkgd', weights.astype(jnp.bfloat16), value_heads, p...]
    all_gather x1 -> x0, waiting for transfers between devices: 53.5 us -> none  [per_device(): every_query = lax.all_gather(queries, 'ctx', axis=0, tiled=True)]
    reduce_sum x11 -> x0, other arithmetic: 49.8 us -> none  [the longest x9 39.7 us: attend_block(): totals = jnp.sum(weights, axis=3)]
    reduce_scatter x1 -> x0, waiting for transfers between devices: 43.3 us -> none  [per_device(): lax.psum_scatter(head_terms, 'tp', scatter_dimension=1, tiled=True)]
    all_gather x2 -> x0, blocking collectives: 42.4 us -> none  [the longest x1 22.3 us: per_device(): lax.all_gather(fresh_keys, 'ctx', axis=0, tiled=True)]
    all_to_all x1 -> x0, blocking collectives: 11.2 us -> none  [per_device(): lax.all_to_all(part_log[None], 'ctx', split_axis=1, concat_axis=0, tiled=...]
  transfers between devices with their start and end apart: 3 -> 0, of which waited for: 2 -> 0; matrix products, arithmetic and copies ran while one was open for 1% -> 0% of each run, Pallas kernels for 0% -> 0%
where the time goes in v1:
time: 74.2 us; the launch traced here: 73 us
  Pallas kernels  70.7 us (95%)
  local copies, waits for them, and re-layouts  1.57 us (2%)
    pallas_call x1, Pallas kernels, per_device(): pl.pallas_call(functools.partial(kernel, grid_ctx, grid_tp), out_shape=ja...  70.7 us
    unnamed x1, local copies, waits for them, and re-layouts  1.57 us

profile of v1, /device:TPU:0, one launch (start us, length us, event | category | flops | bytes accessed | tf_op | source)
XLA Modules:
  0.0 73.0 jit_solution(13328005643546123234)
XLA Ops:
  0.7 70.7 %shard_map.82 = bf16[64,1024]{1,0:T(8,128)(2,1)} custom-call(bf16[64,1024]{1,0:T(8,128)(2,1)} %q_ref.1, bf16[64,128]{1,0:T(8,128)(2,1)} %fk_ref.1, bf16[64,128]{1,0:T(8,128)(2,1)} %fv_ref.1, s32[1,64]{1,0:T(1,128)} %bitcast.1, s32[1]{0:T(128)S(6)} %copy.10.len_ref, bf16[4096,128]{1,0:T(8,128)(2,1)} %k_hbm.1, bf16[4096,128]{1,0:T(8,128)(2,1)} %v_hbm.1, ...), custom_call_target="tpu_custom_call" | custom-call | flops 18790481920 | bytes 18874368 | tf_op jit(solution)/shard_map/pallas_call | solution.py:355
  71.4 1.6 %copy.11 = bf16[64,1024]{1,0:T(8,128)(2,1)} copy(bf16[64,1024]{1,0:T(8,128)(2,1)} %shard_map.82) | data formatting | bytes 262144

commit v2 on v1

--- a/solution.py
+++ b/solution.py
@@ -195,7 +195,7 @@
         fresh[...] = s
         return s
 
-    wide = min(256, block)
+    wide = min(1024, block)
 
     def top_of(s):
         return jnp.max(s.reshape(s.shape[0] // 8, 8, rows), axis=0)

time: 74.2 us -> 73.4 us (0.989)
  Pallas kernels: 70.7 us -> 69.9 us
    pallas_call x1, Pallas kernels: 70.7 us -> 69.9 us  [per_device(): pl.pallas_call(functools.partial(kernel, grid_ctx, grid_tp), out_shape=ja...]
where the time goes in v2:
time: 73.4 us; the launch traced here: 72.1 us
  Pallas kernels  69.9 us (95%)
  local copies, waits for them, and re-layouts  1.57 us (2%)
    pallas_call x1, Pallas kernels, per_device(): pl.pallas_call(functools.partial(kernel, grid_ctx, grid_tp), out_shape=ja...  69.9 us
    unnamed x1, local copies, waits for them, and re-layouts  1.57 us

profile of v2, /device:TPU:0, one launch (start us, length us, event | category | flops | bytes accessed | tf_op | source)
XLA Modules:
  0.0 72.1 jit_solution(14272386736962253204)
XLA Ops:
  0.7 69.9 %shard_map.82 = bf16[64,1024]{1,0:T(8,128)(2,1)} custom-call(bf16[64,1024]{1,0:T(8,128)(2,1)} %q_ref.1, bf16[64,128]{1,0:T(8,128)(2,1)} %fk_ref.1, bf16[64,128]{1,0:T(8,128)(2,1)} %fv_ref.1, s32[1,64]{1,0:T(1,128)} %bitcast.1, s32[1]{0:T(128)S(6)} %copy.10.len_ref, bf16[4096,128]{1,0:T(8,128)(2,1)} %k_hbm.1, bf16[4096,128]{1,0:T(8,128)(2,1)} %v_hbm.1, ...), custom_call_target="tpu_custom_call" | custom-call | flops 18790481920 | bytes 18874368 | tf_op jit(solution)/shard_map/pallas_call | solution.py:355
  70.5 1.6 %copy.11 = bf16[64,1024]{1,0:T(8,128)(2,1)} copy(bf16[64,1024]{1,0:T(8,128)(2,1)} %shard_map.82) | data formatting | bytes 262144

commit v3 on v2

--- a/solution.py
+++ b/solution.py
@@ -34,6 +34,7 @@
     w_hbm,
     out_ref,
     qbuf,
+    q_two,
     meta,
     kbuf,
     vbuf,
@@ -130,7 +131,7 @@
     def proj_copy(k):
         return remote(proj_out.at[k], proj_got.at[k], proj_send.at[k], proj_recv.at[k], {"tp": to_column(k)})
 
-    k_load = pltpu.make_async_copy(k_hbm, kbuf.at[0, pl.ds(0, slots)], local_sem.at[0])
+    k_load = pltpu.make_async_copy(k_hbm, kbuf.at[0, pl.ds(0, slots), pl.ds(0, HEAD)], local_sem.at[0])
     v_load = pltpu.make_async_copy(v_hbm, v_raw, local_sem.at[1])
     w_load = pltpu.make_async_copy(w_hbm, wbuf, local_sem.at[2])
     k_load.start()
@@ -147,7 +148,9 @@
     qbuf[0] = stacked.T.astype(BF16)
     meta[0] = jnp.broadcast_to(jnp.concatenate([pos_ref[...].astype(F32)] * GROUP, axis=1), (8, rows))
     spare = jnp.zeros((FRESH - tokens, HEAD), F32)
-    kbuf[0, pl.ds(slots, FRESH), :] = jnp.concatenate([fk_ref[...].astype(F32), spare], axis=0).astype(BF16)
+    fresh_keys = jnp.concatenate([fk_ref[...].astype(F32), spare], axis=0).astype(BF16)
+    for half in range(2):
+        kbuf[0, pl.ds(slots, FRESH), pl.ds(half * HEAD, HEAD)] = fresh_keys
     vbuf[0, pl.ds(0, HEAD), pl.ds(slots, FRESH)] = (
         jnp.concatenate([fv_ref[...].astype(F32), spare], axis=0).T.astype(BF16)
     )
@@ -163,14 +166,16 @@
 
     filled = len_ref[0]
     k_load.wait()
-    lead = kbuf[0, pl.ds(0, 16), :].astype(F32)[0:1]
+    lead = kbuf[0, pl.ds(0, 16), pl.ds(0, HEAD)].astype(F32)[0:1]
     tidy = block // 2
 
     @pl.loop(0, slots // tidy)
     def _(c):
         at = pl.ds(pl.multiple_of(c * tidy, tidy), tidy)
         valid = lax.broadcasted_iota(jnp.int32, (tidy, HEAD), 0) + c * tidy < filled
-        kbuf[0, at, :] = jnp.where(valid, kbuf[0, at, :].astype(F32), lead).astype(BF16)
+        keys = jnp.where(valid, kbuf[0, at, pl.ds(0, HEAD)].astype(F32), lead).astype(BF16)
+        kbuf[0, at, pl.ds(0, HEAD)] = keys
+        kbuf[0, at, pl.ds(HEAD, HEAD)] = keys
 
     k_partner().start()
     v_load.wait()
@@ -185,12 +190,18 @@
     v_partner().start()
     w_load.start()
 
+    def split_queries(tile):
+        scaled = qbuf[tile].astype(F32) * UNIT
+        high = scaled.astype(BF16)
+        q_two[pl.ds(0, HEAD), :] = high
+        q_two[pl.ds(HEAD, HEAD), :] = (scaled - high.astype(F32)).astype(BF16)
+
     def fresh_scores(tile, shard, fresh):
         row = lax.broadcasted_iota(jnp.int32, (FRESH, FRESH), 0)
         lane = lax.broadcasted_iota(jnp.int32, (FRESH, FRESH), 1)
         spots = jnp.where(row == lane, meta[shard * peers, 0:1, pl.ds(0, FRESH)], 0.0)
         spot = jnp.where(row[:, :1] < tokens, jnp.sum(spots, axis=1, keepdims=True), FAR)
-        s = jnp.dot(kbuf[shard, pl.ds(slots, FRESH), :], qbuf[tile], preferred_element_type=F32)
+        s = jnp.dot(kbuf[shard, pl.ds(slots, FRESH), :], q_two[...], preferred_element_type=F32)
         s = jnp.where(spot <= meta[tile, 0:1, :], s, LOW)
         fresh[...] = s
         return s
@@ -205,10 +216,9 @@
             s_now, f_now = now
             m_old = m_now[0:1, :]
             m_new = jnp.maximum(m_old, jnp.max(peak[...], axis=0, keepdims=True))
-            fade = jnp.exp2((m_old - m_new) * UNIT)
+            fade = jnp.exp2(m_old - m_new)
             m_now[...] = jnp.broadcast_to(m_new, (8, rows))
-            mk = m_new * UNIT
-            p = jnp.exp2(f_now[...] * UNIT - mk).astype(BF16)
+            p = jnp.exp2((f_now[...] - m_new).astype(BF16))
             add = jnp.dot(vbuf[shard_now, :, pl.ds(slots, FRESH)], p, preferred_element_type=F32)
             acc[...] = acc[...] * fade + add
         if then is not None:
@@ -219,11 +229,11 @@
             for c in range(block // wide):
                 start = b * block + c * wide
                 if then is not None:
-                    s = jnp.dot(kbuf[shard_then, pl.ds(start, wide), :], qbuf[tile], preferred_element_type=F32)
+                    s = jnp.dot(kbuf[shard_then, pl.ds(start, wide), :], q_two[...], preferred_element_type=F32)
                     s_then[pl.ds(start, wide), :] = s
                     top = jnp.maximum(top, top_of(s))
                 if now is not None:
-                    weights.append(jnp.exp2(s_now[pl.ds(start, wide), :] * UNIT - mk).astype(BF16))
+                    weights.append(jnp.exp2((s_now[pl.ds(start, wide), :] - m_new).astype(BF16)))
             if now is not None:
                 acc[...] += jnp.dot(
                     vbuf[shard_now, :, pl.ds(b * block, block)],
@@ -240,10 +250,11 @@
     def finish(k):
         total = acc[pl.ds(HEAD, 8), :]
         part_out[k] = (acc[pl.ds(0, HEAD), :] / total[0:1]).astype(BF16)
-        part_log[k] = m_now[...] * UNIT + jnp.log(total) * math.log2(math.e)
+        part_log[k] = m_now[...] + jnp.log(total) * math.log2(math.e)
 
     a, b = (s_a, f_a), (s_b, f_b)
     clear()
+    split_queries(0)
     phase(None, a, 0, None, 0)
 
     @pl.loop(0, peers)
@@ -260,6 +271,7 @@
             q_copy(t + 1).wait_recv()
             meta_copy(t + 1).wait_recv()
 
+        split_queries(tile)
         phase(a, b, tile, shard, shard)
 
         @pl.when(t == 0)
@@ -359,8 +371,9 @@
         out_specs=vmem,
         scratch_shapes=[
             pltpu.VMEM((peers, HEAD, rows), BF16),
+            pltpu.VMEM((2 * HEAD, rows), BF16),
             pltpu.VMEM((peers + 1, 8, rows), F32),
-            pltpu.VMEM((2, slots + FRESH, HEAD), BF16),
+            pltpu.VMEM((2, slots + FRESH, 2 * HEAD), BF16),
             pltpu.VMEM((2, HEAD + ONES, slots + FRESH), BF16),
             pltpu.VMEM((slots, HEAD), BF16),
             pltpu.VMEM(out_weight.shape, BF16),

time: 73.4 us -> 70.9 us (0.966)
  Pallas kernels: 69.9 us -> 67.3 us
    pallas_call x1, Pallas kernels: 69.9 us -> 67.3 us  [per_device(): pl.pallas_call(functools.partial(kernel, grid_ctx, grid_tp), out_shape=ja...]
where the time goes in v3:
time: 70.9 us; the launch traced here: 69.5 us
  Pallas kernels  67.3 us (95%)
  local copies, waits for them, and re-layouts  1.57 us (2%)
    pallas_call x1, Pallas kernels, per_device(): pl.pallas_call(functools.partial(kernel, grid_ctx, grid_tp), out_shape=ja...  67.3 us
    unnamed x1, local copies, waits for them, and re-layouts  1.57 us

profile of v3, /device:TPU:0, one launch (start us, length us, event | category | flops | bytes accessed | tf_op | source)
XLA Modules:
  0.0 69.5 jit_solution(16161126443497724306)
XLA Ops:
  0.7 67.3 %shard_map.82 = bf16[64,1024]{1,0:T(8,128)(2,1)} custom-call(bf16[64,1024]{1,0:T(8,128)(2,1)} %q_ref.1, bf16[64,128]{1,0:T(8,128)(2,1)} %fk_ref.1, bf16[64,128]{1,0:T(8,128)(2,1)} %fv_ref.1, s32[1,64]{1,0:T(1,128)} %bitcast.1, s32[1]{0:T(128)S(6)} %copy.10.len_ref, bf16[4096,128]{1,0:T(8,128)(2,1)} %k_hbm.1, bf16[4096,128]{1,0:T(8,128)(2,1)} %v_hbm.1, ...), custom_call_target="tpu_custom_call" | custom-call | flops 18790481920 | bytes 18874368 | tf_op jit(solution)/shard_map/pallas_call | solution.py:367
  67.9 1.6 %copy.11 = bf16[64,1024]{1,0:T(8,128)(2,1)} copy(bf16[64,1024]{1,0:T(8,128)(2,1)} %shard_map.82) | data formatting | bytes 262144

commit v4 on v3

--- a/solution.py
+++ b/solution.py
@@ -87,12 +87,17 @@
     pz, px = lax.div(tp, tx), lax.rem(tp, tx)
     partner = ctx + 1 - 2 * core
 
-    def to_chip(k):
+    def in_turn(k):
+        return k + (1 - 2 * lax.rem(k, 2)) * lax.div(k + peers - 2, peers)
+
+    def to_chip(turn):
+        k = in_turn(turn)
         z = lax.rem(cz + nz - lax.div(k, ny), nz)
         y = lax.rem(cy + ny - lax.rem(k, ny), ny)
         return (z * ny + y) * 2 + core
 
-    def from_chip(k):
+    def from_chip(turn):
+        k = in_turn(turn)
         z = lax.rem(cz + lax.div(k, ny), nz)
         y = lax.rem(cy + lax.rem(k, ny), ny)
         return (z * ny + y) * 2 + core
@@ -117,7 +122,8 @@
         return remote(meta.at[0], meta.at[peers], meta_send.at[peers], meta_recv.at[peers], {"ctx": partner})
 
     def k_partner():
-        return remote(kbuf.at[0], kbuf.at[1], kv_send.at[0], kv_recv.at[0], {"ctx": partner})
+        half = pl.ds(0, HEAD)
+        return remote(kbuf.at[0, :, half], kbuf.at[1, :, half], kv_send.at[0], kv_recv.at[0], {"ctx": partner})
 
     def v_partner():
         return remote(vbuf.at[0], vbuf.at[1], kv_send.at[1], kv_recv.at[1], {"ctx": partner})
@@ -157,7 +163,7 @@
     vbuf[0, pl.ds(HEAD, ONES), pl.ds(slots, FRESH)] = jnp.ones((ONES, FRESH), BF16)
 
     pl.semaphore_wait(barrier, peers - 1 + 1 + columns - 1)
-    first_sends = min(4, peers)
+    first_sends = min(3, peers)
     for k in range(1, first_sends):
         q_copy(k).start()
     for k in range(1, peers):
@@ -280,6 +286,13 @@
             m_own[...] = m_now[...]
             meta_partner().wait_recv()
             k_partner().wait_recv()
+
+            @pl.loop(0, slots // tidy)
+            def _(c):
+                at = pl.ds(pl.multiple_of(c * tidy, tidy), tidy)
+                kbuf[1, at, pl.ds(HEAD, HEAD)] = kbuf[1, at, pl.ds(0, HEAD)]
+
+            kbuf[1, pl.ds(slots, FRESH), pl.ds(HEAD, HEAD)] = kbuf[1, pl.ds(slots, FRESH), pl.ds(0, HEAD)]
 
         @pl.when(t > 0)
         def _():

time: 70.9 us -> 69.7 us (0.983); the launches traced: 69.5 us -> 69.5 us
  no operation moved by 1% of the time
where the time goes in v4:
time: 69.7 us; the launch traced here: 69.5 us
  Pallas kernels  67.3 us (97%)
  local copies, waits for them, and re-layouts  1.57 us (2%)
    pallas_call x1, Pallas kernels, per_device(): pl.pallas_call(functools.partial(kernel, grid_ctx, grid_tp), out_shape=ja...  67.3 us
    unnamed x1, local copies, waits for them, and re-layouts  1.57 us

profile of v4, /device:TPU:0, one launch (start us, length us, event | category | flops | bytes accessed | tf_op | source)
XLA Modules:
  0.0 69.5 jit_solution(7017006778294872726)
XLA Ops:
  0.7 67.3 %shard_map.82 = bf16[64,1024]{1,0:T(8,128)(2,1)} custom-call(bf16[64,1024]{1,0:T(8,128)(2,1)} %q_ref.1, bf16[64,128]{1,0:T(8,128)(2,1)} %fk_ref.1, bf16[64,128]{1,0:T(8,128)(2,1)} %fv_ref.1, s32[1,64]{1,0:T(1,128)} %bitcast.1, s32[1]{0:T(128)S(6)} %copy.10.len_ref, bf16[4096,128]{1,0:T(8,128)(2,1)} %k_hbm.1, bf16[4096,128]{1,0:T(8,128)(2,1)} %v_hbm.1, ...), custom_call_target="tpu_custom_call" | custom-call | flops 18790481920 | bytes 18874368 | tf_op jit(solution)/shard_map/pallas_call | solution.py:380
  68.0 1.6 %copy.11 = bf16[64,1024]{1,0:T(8,128)(2,1)} copy(bf16[64,1024]{1,0:T(8,128)(2,1)} %shard_map.82) | data formatting | bytes 262144

commit v5 on v4

--- a/solution.py
+++ b/solution.py
@@ -56,6 +56,8 @@
     attended,
     proj_out,
     proj_got,
+    relay_out,
+    relay_got,
     local_sem,
     q_send,
     q_recv,
@@ -69,6 +71,8 @@
     log_recv,
     proj_send,
     proj_recv,
+    relay_send,
+    relay_recv,
 ):
     nz, ny = grid_ctx
     tz, tx = grid_tp
@@ -136,6 +140,11 @@
 
     def proj_copy(k):
         return remote(proj_out.at[k], proj_got.at[k], proj_send.at[k], proj_recv.at[k], {"tp": to_column(k)})
+
+    def relay_copy(dz, side):
+        to = to_column(1 if side == 0 else tx - 1)
+        sems = relay_send.at[2 * dz + side], relay_recv.at[2 * dz + side]
+        return remote(relay_out.at[dz, side], relay_got.at[dz, side], *sems, {"tp": to})
 
     k_load = pltpu.make_async_copy(k_hbm, kbuf.at[0, pl.ds(0, slots), pl.ds(0, HEAD)], local_sem.at[0])
     v_load = pltpu.make_async_copy(v_hbm, v_raw, local_sem.at[1])
@@ -338,14 +347,37 @@
         at = pl.ds(pl.multiple_of(to_column(k) * span, span), span)
         return jnp.dot(attended[...], wbuf[:, at], preferred_element_type=F32)
 
-    @pl.loop(0, columns - 1)
-    def _(s):
-        k = columns - 1 - s
-        proj_out[k] = project(k).astype(BF16)
+    def send_projected(k, terms):
+        proj_out[k] = terms.astype(BF16)
         proj_copy(k).start()
 
+    relayed = tx == 4
+    side_span = span // 2
+    if relayed:
+        direct = [dz * tx for dz in range(tz - 1, 0, -1)]
+        joined = [(dz, side) for dz in range(tz - 1, -1, -1) for side in range(2)]
+        for dz in range(tz - 1, -1, -1):
+            terms = project(dz * tx + 2).astype(BF16)
+            for side in range(2):
+                relay_out[dz, side] = terms[:, side * side_span : (side + 1) * side_span]
+                relay_copy(dz, side).start()
+    else:
+        direct = list(range(columns - 1, 0, -1))
+        joined = []
+    for k in direct:
+        send_projected(k, project(k))
+    for dz, side in joined:
+        k = dz * tx + (1 if side == 0 else tx - 1)
+        terms = project(k)
+        relay_copy(dz, side).wait_recv()
+        left, right = terms[:, :side_span], terms[:, side_span:]
+        more = relay_got[dz, side].astype(F32)
+        halves = [left + more, right] if side == 0 else [left, right + more]
+        send_projected(k, jnp.concatenate(halves, axis=1))
+    sent = direct + [dz * tx + (1 if side == 0 else tx - 1) for dz, side in joined]
+
     result = project(0)
-    for k in range(columns - 1, 0, -1):
+    for k in sent:
         proj_copy(k).wait_recv()
         result += proj_got[k].astype(F32)
     out_ref[...] = result.astype(BF16)
@@ -358,12 +390,14 @@
     meta_partner().wait_send()
     k_partner().wait_send()
     v_partner().wait_send()
-    for k in range(1, columns):
+    for k in sent:
         proj_copy(k).wait_send()
+    for dz, side in joined:
+        relay_copy(dz, side).wait_send()
 
 
 def grid_of(count):
-    return (2, count // 2) if count > 2 else (1, count)
+    return (2, count // 2) if count > 4 else (1, count)
 
 
 def per_device(queries, cache_keys, stored_values, fresh_keys, fresh_values, positions, lengths, out_weight, sizes):
@@ -406,6 +440,8 @@
             pltpu.VMEM((tokens, width), BF16),
             pltpu.VMEM((tp_size, tokens, span), BF16),
             pltpu.VMEM((tp_size, tokens, span), BF16),
+            pltpu.VMEM((grid_tp[0], 2, tokens, span // 2), BF16),
+            pltpu.VMEM((grid_tp[0], 2, tokens, span // 2), BF16),
             dma((3,)),
             dma((peers,)),
             dma((peers,)),
@@ -419,6 +455,8 @@
             dma((peers,)),
             dma((tp_size,)),
             dma((tp_size,)),
+            dma((2 * grid_tp[0],)),
+            dma((2 * grid_tp[0],)),
         ],
         compiler_params=pltpu.CompilerParams(
             collective_id=0, has_side_effects=True, vmem_limit_bytes=60 * 1024 * 1024

time: 69.7 us -> 68.9 us (0.989)
  Pallas kernels: 67.3 us -> 66.5 us
    pallas_call x1, Pallas kernels: 67.3 us -> 66.5 us  [per_device(): pl.pallas_call(functools.partial(kernel, grid_ctx, grid_tp), out_shape=ja...]
where the time goes in v5:
time: 68.9 us; the launch traced here: 68.8 us
  Pallas kernels  66.5 us (97%)
  local copies, waits for them, and re-layouts  1.57 us (2%)
    pallas_call x1, Pallas kernels, per_device(): pl.pallas_call(functools.partial(kernel, grid_ctx, grid_tp), out_shape=ja...  66.5 us
    unnamed x1, local copies, waits for them, and re-layouts  1.57 us

profile of v5, /device:TPU:0, one launch (start us, length us, event | category | flops | bytes accessed | tf_op | source)
XLA Modules:
  0.0 68.8 jit_solution(15933154818974022770)
XLA Ops:
  0.7 66.5 %shard_map.82 = bf16[64,1024]{1,0:T(8,128)(2,1)} custom-call(bf16[64,1024]{1,0:T(8,128)(2,1)} %q_ref.1, bf16[64,128]{1,0:T(8,128)(2,1)} %fk_ref.1, bf16[64,128]{1,0:T(8,128)(2,1)} %fv_ref.1, s32[1,64]{1,0:T(1,128)} %bitcast.1, s32[1]{0:T(128)S(6)} %copy.10.len_ref, bf16[4096,128]{1,0:T(8,128)(2,1)} %k_hbm.1, bf16[4096,128]{1,0:T(8,128)(2,1)} %v_hbm.1, ...), custom_call_target="tpu_custom_call" | custom-call | flops 18790481920 | bytes 18874368 | tf_op jit(solution)/shard_map/pallas_call | solution.py:414
  67.2 1.6 %copy.11 = bf16[64,1024]{1,0:T(8,128)(2,1)} copy(bf16[64,1024]{1,0:T(8,128)(2,1)} %shard_map.82) | data formatting | bytes 262144

commit v6 on v5

--- a/solution.py
+++ b/solution.py
@@ -195,15 +195,11 @@
     k_partner().start()
     v_load.wait()
 
-    @pl.loop(0, slots // tidy)
-    def _(c):
-        at = pl.ds(pl.multiple_of(c * tidy, tidy), tidy)
-        valid = lax.broadcasted_iota(jnp.int32, (HEAD, tidy), 1) + c * tidy < filled
+    def tidy_values(b):
+        at = pl.ds(b * block, block)
+        valid = lax.broadcasted_iota(jnp.int32, (HEAD, block), 1) + b * block < filled
         vbuf[0, pl.ds(0, HEAD), at] = jnp.where(valid, v_raw[at, :].astype(F32).T, 0.0).astype(BF16)
         vbuf[0, pl.ds(HEAD, ONES), at] = jnp.where(valid[:ONES], 1.0, 0.0).astype(BF16)
-
-    v_partner().start()
-    w_load.start()
 
     def split_queries(tile):
         scaled = qbuf[tile].astype(F32) * UNIT
@@ -226,7 +222,7 @@
     def top_of(s):
         return jnp.max(s.reshape(s.shape[0] // 8, 8, rows), axis=0)
 
-    def phase(now, then, tile, shard_now, shard_then):
+    def phase(now, then, tile, shard_now, shard_then, beside=None):
         if now is not None:
             s_now, f_now = now
             m_old = m_now[0:1, :]
@@ -240,6 +236,8 @@
             s_then, f_then = then
             top = top_of(fresh_scores(tile, shard_then, f_then))
         for b in range(BLOCKS):
+            if beside is not None:
+                beside(b)
             weights = []
             for c in range(block // wide):
                 start = b * block + c * wide
@@ -270,7 +268,9 @@
     a, b = (s_a, f_a), (s_b, f_b)
     clear()
     split_queries(0)
-    phase(None, a, 0, None, 0)
+    phase(None, a, 0, None, 0, tidy_values)
+    v_partner().start()
+    w_load.start()
 
     @pl.loop(0, peers)
     def _(t):

time: 68.9 us -> 68.9 us (level)
  no operation moved by 1% of the time
where the time goes in v6:
time: 68.9 us; the launch traced here: 68.8 us
  Pallas kernels  66.5 us (97%)
  local copies, waits for them, and re-layouts  1.57 us (2%)
    pallas_call x1, Pallas kernels, per_device(): pl.pallas_call(functools.partial(kernel, grid_ctx, grid_tp), out_shape=ja...  66.5 us
    unnamed x1, local copies, waits for them, and re-layouts  1.57 us

profile of v6, /device:TPU:0, one launch (start us, length us, event | category | flops | bytes accessed | tf_op | source)
XLA Modules:
  0.0 68.8 jit_solution(5374430634964882648)
XLA Ops:
  0.7 66.5 %shard_map.82 = bf16[64,1024]{1,0:T(8,128)(2,1)} custom-call(bf16[64,1024]{1,0:T(8,128)(2,1)} %q_ref.1, bf16[64,128]{1,0:T(8,128)(2,1)} %fk_ref.1, bf16[64,128]{1,0:T(8,128)(2,1)} %fv_ref.1, s32[1,64]{1,0:T(1,128)} %bitcast.1, s32[1]{0:T(128)S(6)} %copy.10.len_ref, bf16[4096,128]{1,0:T(8,128)(2,1)} %k_hbm.1, bf16[4096,128]{1,0:T(8,128)(2,1)} %v_hbm.1, ...), custom_call_target="tpu_custom_call" | custom-call | flops 18790481920 | bytes 18874368 | tf_op jit(solution)/shard_map/pallas_call | solution.py:414
  67.2 1.6 %copy.11 = bf16[64,1024]{1,0:T(8,128)(2,1)} copy(bf16[64,1024]{1,0:T(8,128)(2,1)} %shard_map.82) | data formatting | bytes 262144

commit v7 on v6

--- a/solution.py
+++ b/solution.py
@@ -11,7 +11,7 @@
 HEAD = 128
 GROUP = 8
 FRESH = 128
-BLOCKS = 4
+BLOCKS = 8
 LOW = -1e30
 FAR = 1e9
 ONES = 16

time: 68.9 us -> 67.1 us (0.974)
  Pallas kernels: 66.5 us -> 64.7 us
    pallas_call x1, Pallas kernels: 66.5 us -> 64.7 us  [per_device(): pl.pallas_call(functools.partial(kernel, grid_ctx, grid_tp), out_shape=ja...]
where the time goes in v7:
time: 67.1 us; the launch traced here: 66.9 us
  Pallas kernels  64.7 us (96%)
  local copies, waits for them, and re-layouts  1.57 us (2%)
    pallas_call x1, Pallas kernels, per_device(): pl.pallas_call(functools.partial(kernel, grid_ctx, grid_tp), out_shape=ja...  64.7 us
    unnamed x1, local copies, waits for them, and re-layouts  1.57 us

profile of v7, /device:TPU:0, one launch (start us, length us, event | category | flops | bytes accessed | tf_op | source)
XLA Modules:
  0.0 66.9 jit_solution(2284459242684694260)
XLA Ops:
  0.7 64.7 %shard_map.82 = bf16[64,1024]{1,0:T(8,128)(2,1)} custom-call(bf16[64,1024]{1,0:T(8,128)(2,1)} %q_ref.1, bf16[64,128]{1,0:T(8,128)(2,1)} %fk_ref.1, bf16[64,128]{1,0:T(8,128)(2,1)} %fv_ref.1, s32[1,64]{1,0:T(1,128)} %bitcast.1, s32[1]{0:T(128)S(6)} %copy.10.len_ref, bf16[4096,128]{1,0:T(8,128)(2,1)} %k_hbm.1, bf16[4096,128]{1,0:T(8,128)(2,1)} %v_hbm.1, ...), custom_call_target="tpu_custom_call" | custom-call | flops 18790481920 | bytes 18874368 | tf_op jit(solution)/shard_map/pallas_call | solution.py:414
  65.4 1.6 %copy.11 = bf16[64,1024]{1,0:T(8,128)(2,1)} copy(bf16[64,1024]{1,0:T(8,128)(2,1)} %shard_map.82) | data formatting | bytes 262144
